TPU v7x, 128 devices: a whole 4x4x4 slice. The times are simulated.
128 devices in a mesh: wide: 16 (over x, z_lo, core), deep: 8 (over z_hi, y).
Axes of the slice: x: 4, y: 4, z: 4 (z_hi: 2, z_lo: 2; z = z_hi * 2 + z_lo), core: 2. Of those that a mesh axis runs over, the one named last changes fastest.
Arguments:
- ocean_level: float32 [512, 1024], P('wide', 'deep'), may hold values from -1.5 to 1.5
- ocean_velocity: float32 [2, 40, 512, 1024], P(None, None, 'wide', 'deep'), may hold values from -1.8 to 1.8
- bathymetry: float32 [512, 1024], P('wide', 'deep'), may hold values from 2 to 6
- sea_mask: int32 [512, 1024], P('wide', 'deep'), may hold values from 0 to 1, as said below
- stress_in: float32 [3, 512, 1024], P(None, 'wide', 'deep'), may hold values from -6 to 6
- spectra: bfloat16 [36, 36, 256, 512], P(None, None, ('wide', 'deep')), may hold values from 0.019897461 to 1
- wind_field: bfloat16 [2, 256, 512], P(None, ('wide', 'deep')), may hold values from -9 to 9
Outputs:
- level_out: float32 [512, 1024], P('wide', 'deep')
- velocity_out: float32 [2, 40, 512, 1024], P(None, None, 'wide', 'deep')
- spectra_out: bfloat16 [36, 36, 256, 512], P(None, None, ('wide', 'deep'))
- stress_out: float32 [3, 256, 512], P(None, 'wide', 'deep')
Inputs may be any that keep to these rules, and one draw needn't show every extreme that they name: `sea_mask`: 1 marks sea, 0 land. In each device's tile of 32 x 128 cells the land is a band of whole columns in the middle of the tile along the second dimension, from local column 64 - 2b to 64 + 2b - 1, with b drawn per tile from 8 to 16, so at most half of a tile is land, and some tile is land in exactly half; blocks of 2 x 2 cells starting at even indices are all sea or all land.
All inputs are finite; a program needn't handle non-finite values.
Results may differ from a plain program's by a relative error of at most 0.009.
Values may be sent and summed in bfloat16 or wider, within the bound.
No kernel may reach another device: no remote copies, remote signals or barrier semaphores. Data moves between devices by JAX's collectives and lax.ppermute only.
A program may use at most 192 MiB of HBM per device.

v0:
```python
import math

import numpy as np

import jax
import jax.numpy as jnp
from jax import lax
from jax.experimental import pallas as pl
from jax.experimental.pallas import tpu as pltpu
from jax.sharding import PartitionSpec as P

LAM_O = 0.2
F_CORIOLIS = 0.1
NU_H = 0.05
KAPPA_V = 0.2
LAM_W = 0.25
GAMMA_BR = 0.73
A_IN = 0.15
C_NL = 0.5
C_WC = 0.002

ND = 36
NF = 36
SIGMA = 0.4 * np.power(1.07, np.arange(NF))
ANGLE = 2.0 * math.pi * np.arange(ND) / ND
TRIG = np.stack([np.cos(ANGLE), np.sin(ANGLE)]).astype(np.float32)

F32 = jnp.float32
BF16 = jnp.bfloat16
VMEM = pltpu.VMEM
SMEM = pltpu.SMEM
HIGH = lax.Precision.HIGHEST


def params(mib):
    return pltpu.CompilerParams(vmem_limit_bytes=mib * 1024 * 1024)


BINS = ND * NF
CELL_ROWS = BINS * 8
PAD = 16
CHUNK = 6


def iotas():
    sub = lax.broadcasted_iota(jnp.int32, (8, 128), 0)
    lane = lax.broadcasted_iota(jnp.int32, (8, 128), 1)
    return sub, lane


def sublane_up(x):
    return pltpu.roll(x, 7, 0)


def sublane_down(x):
    return pltpu.roll(x, 1, 0)


def base_row(d):
    return pl.multiple_of(d * (NF * 8), 8)


def pair_row(ref, start, row):
    return ref[pl.ds(start + row, 8, stride=2), :]


def half_row(d):
    return pl.multiple_of(d * (NF * 4), 16)


HALF_ROWS = BINS * 4


def chunk_copies(source, target, sem):
    def copy(index):
        part = pl.ds(index * CHUNK, CHUNK)
        return pltpu.make_async_copy(source.at[part], target.at[part], sem.at[index])

    return copy


def split_rows_kernel(
    spec_hbm,
    wind_ref,
    upper_hbm,
    lower_hbm,
    held_ref,
    spec_ref,
    turn_ref,
    upper_ref,
    lower_ref,
    sem,
    out_sem,
):
    incoming = chunk_copies(spec_hbm, held_ref, sem)
    chunks = ND // CHUNK

    def outgoing(side, index):
        source, target = ((lower_ref, lower_hbm), (upper_ref, upper_hbm))[side]
        start = pl.multiple_of(index * (CHUNK * NF * 4), 16)
        part = pl.ds(start, CHUNK * NF * 4)
        return pltpu.make_async_copy(source.at[part], target.at[part], out_sem.at[side, index])

    def outgoing_wind(side):
        source, target = ((lower_ref, lower_hbm), (upper_ref, upper_hbm))[side]
        part = pl.ds(HALF_ROWS, 16)
        return pltpu.make_async_copy(source.at[part], target.at[part], out_sem.at[side, chunks])

    for index in range(ND // CHUNK):
        incoming(index).start()
    turn_ref[0:16, :] = wind_ref[...].astype(F32)
    sides = ((0, lower_ref), (1, upper_ref))
    for row, ref in sides:
        wind = jnp.concatenate([pair_row(turn_ref, 0, row), jnp.zeros((8, 128), F32)], axis=0)
        ref[HALF_ROWS:, :] = wind.astype(BF16)
        outgoing_wind(row).start()

    def body(d, carry):
        @pl.when(lax.rem(d, CHUNK) == 0)
        def _():
            incoming(lax.div(d, CHUNK)).wait()

        base = base_row(d)
        for quad in range(NF // 4):
            block = held_ref[d, 32 * quad : 32 * quad + 32, :].astype(F32)
            spec_ref[pl.ds(base + 32 * quad, 32), :] = block
        for quad in range(NF // 4):
            start = base + 32 * quad
            for row, ref in sides:
                halves = [pair_row(spec_ref, start + 16 * pair, row) for pair in range(2)]
                packed = jnp.concatenate(halves, axis=0).astype(BF16)
                ref[pl.ds(half_row(d) + 16 * quad, 16), :] = packed

        @pl.when(lax.rem(d, CHUNK) == CHUNK - 1)
        def _():
            for side in range(2):
                outgoing(side, lax.div(d, CHUNK)).start()

        return carry

    lax.fori_loop(0, ND, body, 0)
    for side in range(2):
        outgoing_wind(side).wait()
        for index in range(chunks):
            outgoing(side, index).wait()


def split_rows(spec, wind):
    half = jax.ShapeDtypeStruct((HALF_ROWS + 16, 128), BF16)
    return pl.pallas_call(
        split_rows_kernel,
        out_shape=(half, half),
        in_specs=[pl.BlockSpec(memory_space=pltpu.HBM), pl.BlockSpec(memory_space=VMEM)],
        out_specs=(pl.BlockSpec(memory_space=pl.ANY),) * 2,
        scratch_shapes=[
            VMEM(spec.shape, BF16),
            VMEM((CELL_ROWS + PAD, 128), F32),
            VMEM((16 + PAD, 128), F32),
            VMEM(half.shape, BF16),
            VMEM(half.shape, BF16),
            pltpu.SemaphoreType.DMA((ND // CHUNK,)),
            pltpu.SemaphoreType.DMA((2, ND // CHUNK + 1)),
        ],
        compiler_params=params(56),
        cost_estimate=pl.CostEstimate(flops=4000000, bytes_accessed=9000000, transcendentals=0),
        name="split_rows",
    )(spec, wind)


FIELDS = 12


def edge_columns(planes):
    lane = lax.broadcasted_iota(jnp.int32, (32, 128), 1)
    first = jnp.zeros((32, 128), F32)
    last = jnp.zeros((32, 128), F32)
    for index, plane in enumerate(planes):
        here = lane == index
        first = jnp.where(here, pltpu.roll(plane, index, 1), first)
        last = jnp.where(here, pltpu.roll(plane, (index + 1) % 128, 1), last)
    return first, last


def gather_kernel(
    level_ref,
    vel_ref,
    bathy_ref,
    mask_ref,
    stress_ref,
    own_hbm,
    low_hbm,
    high_hbm,
    first_ref,
    last_ref,
    own_ref,
    low_ref,
    high_ref,
    sem,
):
    levels = vel_ref.shape[1]
    fields = [
        level_ref[...],
        bathy_ref[...],
        mask_ref[...].astype(F32),
        stress_ref[0],
        stress_ref[1],
        stress_ref[2],
        vel_ref[0, 0],
        vel_ref[1, 0],
        vel_ref[0, 1],
        vel_ref[1, 1],
    ]
    for c in range(2):
        total = vel_ref[c, 0]
        for k in range(1, levels):
            total = total + vel_ref[c, k]
        fields.append(total * (1.0 / levels))
    for index, field in enumerate(fields):
        own_ref[index] = field
        low_ref[index] = field[0:8]
        high_ref[index] = field[24:32]
    blocks = levels // 8
    for c in range(2):
        part = slice(FIELDS + blocks * c, FIELDS + blocks * c + blocks)
        low_ref[part] = vel_ref[c, :, 0, :].reshape(blocks, 8, 128)
        high_ref[part] = vel_ref[c, :, 31, :].reshape(blocks, 8, 128)
    pairs = ((own_ref, own_hbm), (low_ref, low_hbm), (high_ref, high_hbm))
    copies = [pltpu.make_async_copy(*pair, sem.at[i]) for i, pair in enumerate(pairs)]
    for copy in copies:
        copy.start()
    planes = [vel_ref[c, k] for c in range(2) for k in range(levels)]
    planes += [fields[0], fields[4], fields[5], (fields[0] + fields[1]) * fields[11]]
    first_ref[...], last_ref[...] = edge_columns(planes)
    for copy in copies:
        copy.wait()


def gather_surface(level, vel, bathy, mask, stress):
    rows, cols = level.shape
    edge = jax.ShapeDtypeStruct((FIELDS + vel.shape[1] // 4, 8, cols), F32)
    column = jax.ShapeDtypeStruct((rows, cols), F32)
    return pl.pallas_call(
        gather_kernel,
        out_shape=(jax.ShapeDtypeStruct((FIELDS, rows, cols), F32), edge, edge, column, column),
        in_specs=[pl.BlockSpec(memory_space=VMEM)] * 5,
        out_specs=(pl.BlockSpec(memory_space=pl.ANY),) * 3
        + (pl.BlockSpec(memory_space=VMEM),) * 2,
        scratch_shapes=[
            VMEM((FIELDS, rows, cols), F32),
            VMEM(edge.shape, F32),
            VMEM(edge.shape, F32),
            pltpu.SemaphoreType.DMA((3,)),
        ],
        compiler_params=params(56),
        cost_estimate=pl.CostEstimate(flops=400000, bytes_accessed=1700000, transcendentals=0),
        name="gather_surface",
    )(level, vel, bathy, mask, stress)


EXT = 48
ROWS_SENT = 6
EDGE_AT = 4 * ROWS_SENT
COLUMNS_AT = 40
SENT_ROWS = COLUMNS_AT + 32


def surface_kernel(place_ref, own_ref, low_ref, high_ref, first_ref, last_ref, out_ref):
    lane = lax.broadcasted_iota(jnp.int32, (EXT, 128), 1)

    def field(index):
        return jnp.concatenate([low_ref[index], own_ref[index], high_ref[index]], axis=0)

    level, bathy, wet, sxx, sxy, syy, u, v, u1, v1, ubar, vbar = [field(i) for i in range(FIELDS)]

    def down(x):
        return pltpu.roll(x, 1, 0)

    def up(x):
        return pltpu.roll(x, EXT - 1, 0)

    def left(x):
        return jnp.where(lane == 0, 0.0, pltpu.roll(x, 1, 1))

    def right(x):
        return jnp.where(lane == 127, 0.0, pltpu.roll(x, 127, 1))

    depth = bathy + level
    inverse = 1.0 / jnp.where(depth > 0.0, depth, 1.0)
    flux_x = depth * ubar
    flux_y = depth * vbar
    divergence = up(flux_x) - down(flux_x) + right(flux_y) - left(flux_y)
    new_depth = bathy + (level - 0.5 * LAM_O * wet * divergence)
    grad_x = 0.5 * (up(level) - down(level))
    grad_y = 0.5 * (right(level) - left(level))
    force_x = -0.5 * (up(sxx) - down(sxx) + (right(sxy) - left(sxy))) * inverse
    force_y = -0.5 * (up(sxy) - down(sxy) + (right(syy) - left(syy))) * inverse
    laplace_u = up(u) + down(u) + right(u) + left(u) - 4.0 * u
    laplace_v = up(v) + down(v) + right(v) + left(v) - 4.0 * v
    new_u = wet * (
        u
        - LAM_O * grad_x
        + F_CORIOLIS * v
        + LAM_O * force_x
        + NU_H * laplace_u
        + KAPPA_V * (u1 - u)
    )
    new_v = wet * (
        v
        - LAM_O * grad_y
        - F_CORIOLIS * u
        + LAM_O * force_y
        + NU_H * laplace_v
        + KAPPA_V * (v1 - v)
    )

    column = lax.broadcasted_iota(jnp.int32, (128, 128), 0)
    target = lax.broadcasted_iota(jnp.int32, (128, 128), 1)
    to_coarse = jnp.where(target == 64 * (place_ref[0] & 1) + (column >> 1), 0.25, 0.0)
    coarse_row = lax.broadcasted_iota(jnp.int32, (24, EXT), 0)
    fine_row = lax.broadcasted_iota(jnp.int32, (24, EXT), 1)
    pair_sum = jnp.where((fine_row >> 1) == coarse_row, 1.0, 0.0)
    stacked = jnp.concatenate([new_u, new_v, new_depth, wet], axis=0)
    narrowed = jnp.dot(stacked, to_coarse, precision=HIGH, preferred_element_type=F32)
    for index in range(4):
        coarse = jnp.dot(
            pair_sum,
            narrowed[EXT * index : EXT * index + EXT],
            precision=HIGH,
            preferred_element_type=F32,
        )
        for strip in range(8):
            first = 2 * strip + 2
            rows = slice(ROWS_SENT * index, ROWS_SENT * index + ROWS_SENT)
            out_ref[strip, rows, :] = coarse[first : first + ROWS_SENT]

    wet_inverse = wet * inverse
    to_right = [u, v, sxy, syy, level, flux_y]
    to_left = [u, v, -sxy, -syy, -level, -flux_y]
    weights = [
        NU_H * wet,
        NU_H * wet,
        0.5 * LAM_O * wet_inverse,
        0.5 * LAM_O * wet_inverse,
        0.5 * LAM_O * wet,
        0.5 * LAM_O * wet,
    ]
    edges = jnp.zeros((EXT, 128), F32)
    for index in range(6):
        edges = jnp.where(lane == index, to_right[index][:, 127:128], edges)
        edges = jnp.where(lane == 8 + index, to_left[index][:, 0:1], edges)
        edges = jnp.where(lane == 16 + index, weights[index][:, 0:1], edges)
        edges = jnp.where(lane == 24 + index, weights[index][:, 127:128], edges)
    for strip in range(8):
        first = 4 * strip + 4
        rows = 2 * ROWS_SENT
        out_ref[strip, EDGE_AT : EDGE_AT + rows, :] = edges[first : first + rows]
        blank = jnp.zeros((COLUMNS_AT - EDGE_AT - rows, 128), F32)
        out_ref[strip, EDGE_AT + rows : COLUMNS_AT, :] = blank
        columns = jnp.where(place_ref[0] == strip - 1, last_ref[...], 0.0)
        columns = jnp.where(place_ref[0] == strip + 1, first_ref[...], columns)
        out_ref[strip, COLUMNS_AT:, :] = columns


def surface_step(place, *operands):
    return pl.pallas_call(
        surface_kernel,
        out_shape=jax.ShapeDtypeStruct((8, SENT_ROWS, 128), F32),
        in_specs=[pl.BlockSpec(memory_space=SMEM)] + [pl.BlockSpec(memory_space=VMEM)] * 5,
        out_specs=pl.BlockSpec(memory_space=VMEM),
        compiler_params=params(16),
        cost_estimate=pl.CostEstimate(flops=2000000, bytes_accessed=400000, transcendentals=0),
        name="surface_step",
    )(place, *operands)


def rounded(x):
    return x.astype(BF16).astype(F32)


def strip_fields(arrived_ref):
    sub, lane = iotas()
    even = (sub & 1) == 0
    base = 64 * (sub & 1)
    edge_sums = []
    for row in range(ROWS_SENT):
        total = None
        for fine in (2 * row, 2 * row + 1):
            edge = arrived_ref[:, EDGE_AT + fine, :]
            from_left = jnp.where(sub == 0, 0.0, sublane_down(edge))
            from_right = jnp.where(sub == 7, 0.0, sublane_up(edge))
            weight = pltpu.roll(edge, 112, 1)
            product = weight * jnp.where(lane < 8, from_left, from_right)
            total = product if total is None else total + product
        edge_sums.append(0.25 * total)

    def tiles(index, row, parts):
        value = arrived_ref[:, ROWS_SENT * index + row + 2, :]
        if parts:
            edge = edge_sums[row + 2]
            left = sum(edge[:, p : p + 1] for p in parts)
            right = sum(edge[:, 8 + p : 9 + p] for p in parts)
            value = value + jnp.where(lane == base, left, 0.0)
            value = value + jnp.where(lane == base + 63, right, 0.0)
        return value

    def field(index, parts):
        def of_rows(first_row, second_row):
            first = tiles(index, first_row, parts)
            second = tiles(index, second_row, parts)
            return jnp.where(even, first + sublane_up(first), second + sublane_down(second))

        return of_rows

    sums = [field(0, (0, 2)), field(1, (1, 3, 4)), field(2, (5,)), field(3, ())]
    u, v, depth = [lambda a, b, get=get: rounded(get(a, b)) for get in sums[:3]]
    return u, v, depth, lambda a, b: jnp.where(sums[3](a, b) > 0.5, 1.0, 0.0)


def propagate_direction(d, trig_ref, rows_of, faces_x, cells, speed_ref, emit):
    first_lane, last_lane, inside, border, face_v, edge_v, half_wet = cells
    along_x = trig_ref[0, d]
    along_y = trig_ref[1, d] * inside
    along_border = trig_ref[1, d] * border
    for quad in range(NF // 4):
        results = []
        for part, (faces, rows) in enumerate(rows_of(d, quad)):
            speed = speed_ref[2 * quad + part]
            speed_x = along_x * speed
            speed_y = along_y * speed
            speed_border = along_border * speed
            flux_x = []
            for (lower, upper), face in zip(faces, faces_x):
                through = speed_x + face
                flux_x.append(through * jnp.where(through > 0.0, lower, upper))
            moved = []
            for row, (here, beyond, entry, exit) in enumerate(rows):
                through = speed_y + face_v[row]
                following = pltpu.roll(jnp.where(first_lane, beyond, here), 127, 1)
                flux = through * jnp.where(through > 0.0, here, following)
                before = pltpu.roll(jnp.where(last_lane, sublane_down(flux), flux), 1, 1)
                lost = jnp.minimum(speed_border + edge_v[row], 0.0) * here
                change = here + (before - flux) + lost
                if entry is not None:
                    change = change + flux_x[entry]
                if exit is not None:
                    change = change - flux_x[exit]
                moved.append(half_wet[row] * change)
            results.append(moved)
        emit(d, quad, results)


def finish_direction(d, trig_ref, rows_of, faces_x, half_wet, speed_ref, emit):
    along_x = trig_ref[0, d]
    for quad in range(NF // 4):
        results = []
        for part, (below, first, second, above, moved) in enumerate(rows_of(d, quad)):
            speed_x = along_x * speed_ref[2 * quad + part]
            through = speed_x + faces_x[0]
            flux_in = through * jnp.where(through > 0.0, below, first)
            through = speed_x + faces_x[1]
            flux_out = through * jnp.where(through > 0.0, second, above)
            results.append([moved[0] + half_wet[0] * flux_in, moved[1] - half_wet[1] * flux_out])
        emit(d, quad, results)


def source_direction(d, trig_ref, moved_ref, damp_ref, rel_x, rel_y, breaking, emit):
    base = base_row(d)
    plus = base_row(lax.rem(d + 2, ND))
    minus = base_row(lax.rem(d + ND - 2, ND))
    wind_along = A_IN * (rel_x * trig_ref[0, d] + rel_y * trig_ref[1, d])
    spreads = {}

    def spread(f):
        if f not in spreads:
            spreads[f] = moved_ref[pl.ds(plus + 8 * f, 8), :] + moved_ref[pl.ds(minus + 8 * f, 8), :]
        return spreads[f]

    for quad in range(NF // 4):
        results = []
        for part in range(4):
            f = 4 * quad + part
            here = moved_ref[pl.ds(base + 8 * f, 8), :]
            growth = jnp.minimum(jnp.maximum(wind_along * float(SIGMA[f]), A_IN), 3.0 * A_IN)
            summed = (growth + damp_ref[f] - here) * here
            if 0 < f < NF - 1:
                summed = summed + (0.5 * C_NL) * spread(f + 1) * spread(f - 1)
            results.append(summed * breaking)
        emit(quad, results)


def by_row(turn_ref, index, field):
    turn_ref[16 * index : 16 * index + 8] = field
    turn_ref[16 * index + 8 : 16 * index + 16] = field
    return [pair_row(turn_ref, 16 * index, row) for row in range(2)]


def pass_cells(turn_ref, v, wet):
    sub, lane = iotas()
    first_lane, last_lane = lane == 0, lane == 127
    block = sub & 3
    inside = jnp.where(last_lane & (block == 3), 0.0, 1.0)
    border = jnp.where(
        first_lane & (block == 0), 1.0, jnp.where(last_lane & (block == 3), -1.0, 0.0)
    )
    half = 0.5 * LAM_W
    face_v, edge_v = [], []
    for v_row in by_row(turn_ref, 0, v):
        after_v = pltpu.roll(jnp.where(first_lane, sublane_up(v_row), v_row), 127, 1)
        face_v.append(inside * (half * (v_row + after_v)))
        edge_v.append(border * (half * v_row))
    half_wet = [0.5 * wet_row for wet_row in by_row(turn_ref, 1, wet)]
    return first_lane, last_lane, inside, border, face_v, edge_v, half_wet


def set_speeds(speed_ref):
    sub, _ = iotas()
    for pair in range(NF // 2):
        low, high = [float(LAM_W * 0.5 / SIGMA[2 * pair + i]) for i in range(2)]
        speed_ref[pair] = jnp.where(sub < 4, low, high)


def each_direction(body):
    lax.fori_loop(0, ND, lambda d, carry: body(d) or carry, 0)


def summing(moved_ref, sums_ref):
    for f in range(NF):
        sums_ref[f] = jnp.zeros((8, 128), F32)

    def emit(d, quad, results):
        for part, moved in enumerate(results):
            pair = 2 * quad + part
            for row in range(2):
                moved_ref[pl.ds(base_row(d) + 16 * pair + row, 8, stride=2), :] = moved[row]
                sums_ref[2 * pair + row] += moved[row]

    return emit


def packing(refs):
    def emit(d, quad, results):
        for row, ref in enumerate(refs):
            block = jnp.concatenate([moved[row] for moved in results], axis=0)
            ref[pl.ds(half_row(d) + 16 * quad, 16), :] = block.astype(BF16)

    return emit


def source_pass(trig_ref, u, v, depth, wet, wind, scratch, emit, initial=0, combine=None):
    moved_ref, damp_ref, sums_ref, turn_ref = scratch
    sub, _ = iotas()
    zeros = jnp.zeros((8, 128), F32)
    for row in range(2):
        zeroth, second = zeros, zeros
        for pair in range(NF // 2):
            low, high = [float(SIGMA[2 * pair + i] ** 2) for i in range(2)]
            zeroth = zeroth + sums_ref[2 * pair + row]
            second = second + sums_ref[2 * pair + row] * jnp.where(sub < 4, low, high)
        for index, value in ((2, zeroth), (3, second)):
            turn_ref[pl.ds(16 * index + row, 8, stride=2), :] = value + pltpu.roll(value, 4, 0)
    moment_zero = turn_ref[32:40] * (2.0 / BINS)
    moment_two = turn_ref[48:56] * (2.0 / BINS)
    limit = (GAMMA_BR * depth) * (GAMMA_BR * depth)
    breaking = jnp.where(wet > 0.5, 2.0 * limit / jnp.maximum(16.0 * moment_zero, limit), 0.0)
    for f in range(NF):
        damp_ref[f] = (1.0 - A_IN) - float(C_WC * SIGMA[f] ** 3) * moment_two
    rel_x = wind[0] - u
    rel_y = wind[1] - v

    def source(d, carried):
        parts = []
        source_direction(
            d,
            trig_ref,
            moved_ref,
            damp_ref,
            rel_x,
            rel_y,
            breaking,
            lambda quad, results: parts.append(emit(d, quad, results)),
        )
        return combine(d, carried, parts) if combine else carried

    return lax.fori_loop(0, ND, source, initial)


def packed_rows(refs, d, quad):
    blocks = [ref[pl.ds(half_row(d) + 16 * quad, 16), :].astype(F32) for ref in refs]
    return [[block[8 * part : 8 * part + 8] for block in blocks] for part in range(2)]


def wave_scratch():
    return [
        VMEM((CELL_ROWS + PAD, 128), F32),
        VMEM((NF, 8, 128), F32),
        VMEM((NF, 8, 128), F32),
        VMEM((64 + PAD, 128), F32),
        VMEM((NF // 2, 8, 128), F32),
    ]


def inner_rows(refs, d, quad):
    return [
        (
            [(lower, upper)],
            [(lower, sublane_up(lower), None, 0), (upper, sublane_up(upper), 0, None)],
        )
        for lower, upper in packed_rows(refs, d, quad)
    ]


def begin_kernel(
    trig_ref, upper_ref, lower_ref, arrived_ref, part_lower_ref, part_upper_ref, turn_ref, speed_ref
):
    u, v, _, wet = strip_fields(arrived_ref)
    own = by_row(turn_ref, 0, u(0, 1))
    face_own = (0.5 * LAM_W) * (own[0] + own[1])
    set_speeds(speed_ref)
    cells = pass_cells(turn_ref, v(0, 1), wet(0, 1))

    def rows_own(d, quad):
        return inner_rows((lower_ref, upper_ref), d, quad)

    emit = packing((part_lower_ref, part_upper_ref))
    each_direction(
        lambda d: propagate_direction(d, trig_ref, rows_own, (face_own,), cells, speed_ref, emit)
    )


def begin_step(trig, *operands):
    here = pl.BlockSpec(memory_space=VMEM)
    return pl.pallas_call(
        begin_kernel,
        out_shape=(jax.ShapeDtypeStruct((HALF_ROWS, 128), BF16),) * 2,
        in_specs=[pl.BlockSpec(memory_space=SMEM)] + [here] * len(operands),
        out_specs=(here,) * 2,
        scratch_shapes=wave_scratch()[-2:],
        compiler_params=params(16),
        cost_estimate=pl.CostEstimate(
            flops=100000000, bytes_accessed=20000000, transcendentals=0
        ),
        name="begin_wave_step",
    )(trig, *operands)


KEPT = 20


def first_kernel(
    trig_ref,
    upper_ref,
    lower_ref,
    above_ref,
    below_ref,
    part_lower_ref,
    part_upper_ref,
    arrived_ref,
    wind_ref,
    spec_lower_ref,
    spec_upper_ref,
    near_above_ref,
    near_below_ref,
    next_lower_ref,
    next_upper_ref,
    above_out_ref,
    below_out_ref,
    fields_ref,
    spec_ref,
    *scratch,
):
    moved_ref, damp_ref, sums_ref, turn_ref, speed_ref = scratch
    u, v, depth, wet = strip_fields(arrived_ref)
    u_own, u_near = u(0, 1), u(-1, 2)
    own = by_row(turn_ref, 0, u_own)
    near = by_row(turn_ref, 1, u_near)
    half = 0.5 * LAM_W
    face_low = half * (near[0] + own[0])
    face_own = half * (own[0] + own[1])
    face_high = half * (own[1] + near[1])
    wind = wind_ref[...].astype(F32)
    set_speeds(speed_ref)
    v_own, wet_own = v(0, 1), wet(0, 1)
    cells = pass_cells(turn_ref, v_own, wet_own)

    above_out_ref[...] = above_ref[0:HALF_ROWS, :]
    below_out_ref[...] = below_ref[0:HALF_ROWS, :]
    far = by_row(turn_ref, 2, u(-2, 3))
    wet_near = wet(-1, 2)
    for row, ref in ((0, above_ref), (1, below_ref)):
        arrived_wind = ref[HALF_ROWS:, :].astype(F32)[0:8]
        turn_ref[pl.ds(48 + row, 8, stride=2), :] = arrived_wind
    kept = [half * (far[0] + near[0]), half * (near[1] + far[1]), face_low, face_high]
    kept += [u_near, v(-1, 2), depth(-1, 2), wet_near, turn_ref[48:56], turn_ref[56:64]]
    kept += [u_own, v_own, depth(0, 1), wet_own, wind[0:8], wind[8:16]]
    kept += [0.5 * row for field in (wet_near, wet_own) for row in by_row(turn_ref, 0, field)]
    for index, field in enumerate(kept):
        fields_ref[index] = field

    def rows_first(d, quad):
        refs = (above_ref, lower_ref, upper_ref, below_ref, part_lower_ref, part_upper_ref)
        return [(*rows[:4], rows[4:]) for rows in packed_rows(refs, d, quad)]

    emit = summing(moved_ref, sums_ref)
    faces = (face_low, face_high)
    half_own = cells[-1]
    each_direction(
        lambda d: finish_direction(d, trig_ref, rows_first, faces, half_own, speed_ref, emit)
    )

    def emit_spec(d, quad, results):
        start = base_row(d) + 32 * quad
        spec_ref[pl.ds(start, 32), :] = jnp.concatenate(results, axis=0)
        for row, ref in ((0, spec_lower_ref), (1, spec_upper_ref)):
            halves = [pair_row(spec_ref, start + 16 * pair, row) for pair in range(2)]
            packed = jnp.concatenate(halves, axis=0).astype(BF16)
            ref[pl.ds(half_row(d) + 16 * quad, 16), :] = packed

    source_pass(
        trig_ref,
        u_own,
        v_own,
        depth(0, 1),
        wet_own,
        (wind[0:8], wind[8:16]),
        (moved_ref, damp_ref, sums_ref, turn_ref),
        emit_spec,
    )

    def rows_second(d, quad):
        return inner_rows((spec_lower_ref, spec_upper_ref), d, quad)

    emit_next = packing((next_lower_ref, next_upper_ref))
    each_direction(
        lambda d: propagate_direction(
            d, trig_ref, rows_second, (face_own,), cells, speed_ref, emit_next
        )
    )

    cells_near = pass_cells(turn_ref, v(-1, 2), wet(-1, 2))

    def rows_near(d, quad):
        return [
            (
                [(above, lower), (upper, below)],
                [(above, sublane_up(above), None, 0), (below, sublane_up(below), 1, None)],
            )
            for above, lower, upper, below in packed_rows(
                (above_ref, lower_ref, upper_ref, below_ref), d, quad
            )
        ]

    emit_near = packing((near_above_ref, near_below_ref))
    each_direction(
        lambda d: propagate_direction(
            d, trig_ref, rows_near, (face_low, face_high), cells_near, speed_ref, emit_near
        )
    )


def second_kernel(
    trig_ref,
    far_above_ref,
    far_below_ref,
    spec_lower_ref,
    spec_upper_ref,
    near_above_ref,
    near_below_ref,
    next_lower_ref,
    next_upper_ref,
    above_ref,
    below_ref,
    fields_ref,
    out_hbm,
    stress_hbm,
    near_ref,
    out_ref,
    sem,
    stress_ref,
    stress_sem,
    *scratch,
):
    moved_ref, damp_ref, sums_ref, turn_ref, speed_ref = scratch
    shared = (moved_ref, damp_ref, sums_ref, turn_ref)
    kept = [fields_ref[index] for index in range(KEPT)]
    faces_near, faces_own = kept[0:2], kept[2:4]
    half_near, half_own = kept[16:18], kept[18:20]
    set_speeds(speed_ref)

    def rows_near(d, quad):
        refs = (far_above_ref, above_ref, below_ref, far_below_ref, near_above_ref, near_below_ref)
        return [(*rows[:4], rows[4:]) for rows in packed_rows(refs, d, quad)]

    emit = summing(moved_ref, sums_ref)
    each_direction(
        lambda d: finish_direction(d, trig_ref, rows_near, faces_near, half_near, speed_ref, emit)
    )

    def emit_near(d, quad, results):
        near_ref[pl.ds(base_row(d) + 32 * quad, 32), :] = jnp.concatenate(results, axis=0)

    source_pass(trig_ref, *kept[4:8], kept[8:10], shared, emit_near)

    def rows_own(d, quad):
        refs = (spec_lower_ref, spec_upper_ref, next_lower_ref, next_upper_ref)
        parts = []
        for part, rows in enumerate(packed_rows(refs, d, quad)):
            start = base_row(d) + 32 * quad + 16 * part
            below, above = [pair_row(near_ref, start, row) for row in range(2)]
            parts.append((below, rows[0], rows[1], above, rows[2:]))
        return parts

    emit = summing(moved_ref, sums_ref)
    each_direction(
        lambda d: finish_direction(d, trig_ref, rows_own, faces_own, half_own, speed_ref, emit)
    )
    outgoing = chunk_copies(out_ref, out_hbm, sem)
    zeros = jnp.zeros((8, 128), F32)

    def emit_own(d, quad, results):
        packed = jnp.concatenate(results, axis=0).astype(BF16)
        out_ref[d, 32 * quad : 32 * quad + 32, :] = packed
        scales = [float(math.pi / ND * SIGMA[4 * quad + part] / NF) for part in range(4)]
        return sum(result * scale for result, scale in zip(results, scales))

    def add_stress(d, totals, parts):
        @pl.when(lax.rem(d, CHUNK) == CHUNK - 1)
        def _():
            outgoing(lax.div(d, CHUNK)).start()

        total = sum(parts)
        cos_d, sin_d = trig_ref[0, d], trig_ref[1, d]
        xx, xy, yy = totals
        return (
            xx + total * (cos_d * cos_d),
            xy + total * (cos_d * sin_d),
            yy + total * (sin_d * sin_d),
        )

    totals = source_pass(
        trig_ref,
        *kept[10:14],
        kept[14:16],
        shared,
        emit_own,
        (zeros, zeros, zeros),
        add_stress,
    )
    for c in range(3):
        for tile in range(8):
            part = tile // 2
            stress_ref[tile, 2 * c : 2 * c + 2, :] = totals[c][2 * part : 2 * part + 2]
    stress_copy = pltpu.make_async_copy(stress_ref, stress_hbm, stress_sem)
    stress_copy.start()
    for index in range(ND // CHUNK):
        outgoing(index).wait()
    stress_copy.wait()


def first_step(trig, *operands):
    here = pl.BlockSpec(memory_space=VMEM)
    return pl.pallas_call(
        first_kernel,
        out_shape=(jax.ShapeDtypeStruct((HALF_ROWS, 128), BF16),) * 8
        + (jax.ShapeDtypeStruct((KEPT, 8, 128), F32),),
        in_specs=[pl.BlockSpec(memory_space=SMEM)] + [here] * len(operands),
        out_specs=(here,) * 9,
        scratch_shapes=[VMEM((CELL_ROWS + PAD, 128), F32)] + wave_scratch(),
        compiler_params=params(32),
        cost_estimate=pl.CostEstimate(
            flops=100000000, bytes_accessed=60000000, transcendentals=0
        ),
        name="first_wave_step",
    )(trig, *operands)


def second_step(trig, *operands):
    here = pl.BlockSpec(memory_space=VMEM)
    full = jax.ShapeDtypeStruct((ND, NF * 8, 128), BF16)
    return pl.pallas_call(
        second_kernel,
        out_shape=(full, jax.ShapeDtypeStruct((8, 6, 128), F32)),
        in_specs=[pl.BlockSpec(memory_space=SMEM)] + [here] * len(operands),
        out_specs=(pl.BlockSpec(memory_space=pl.ANY),) * 2,
        scratch_shapes=[
            VMEM((CELL_ROWS + PAD, 128), F32),
            VMEM(full.shape, BF16),
            pltpu.SemaphoreType.DMA((ND // CHUNK,)),
            VMEM((8, 6, 128), F32),
            pltpu.SemaphoreType.DMA,
        ]
        + wave_scratch(),
        compiler_params=params(36),
        cost_estimate=pl.CostEstimate(
            flops=200000000, bytes_accessed=40000000, transcendentals=0
        ),
        name="second_wave_step",
    )(trig, *operands)


def ocean_kernel(place_ref, vel_ref, own_ref, low_ref, high_ref, arrived_ref, out_ref, level_ref):
    row = lax.broadcasted_iota(jnp.int32, (32, 128), 0)
    lane = lax.broadcasted_iota(jnp.int32, (32, 128), 1)
    first_row, last_row = row == 0, row == 31
    first_lane, last_lane = lane == 0, lane == 127
    levels = vel_ref.shape[1]
    place = place_ref[0]
    before = arrived_ref[jnp.maximum(place - 1, 0), COLUMNS_AT:, :]
    before = jnp.where(place > 0, before, 0.0)
    after = arrived_ref[jnp.minimum(place + 1, 7), COLUMNS_AT:, :]
    after = jnp.where(place < 7, after, 0.0)

    def down(x, edge):
        return jnp.where(first_row, edge, pltpu.roll(x, 1, 0))

    def up(x, edge):
        return jnp.where(last_row, edge, pltpu.roll(x, 31, 0))

    def left(x, index):
        return jnp.where(first_lane, before[:, index : index + 1], pltpu.roll(x, 1, 1))

    def right(x, index):
        return jnp.where(last_lane, after[:, index : index + 1], pltpu.roll(x, 127, 1))

    def edge_rows(index):
        return low_ref[index, 7:8, :], high_ref[index, 0:1, :]

    level, bathy, wet, sxx, sxy, syy = [own_ref[i] for i in range(6)]
    ubar, vbar = own_ref[10], own_ref[11]
    edges = [edge_rows(i) for i in range(FIELDS)]
    plane_count = 2 * levels
    depth = bathy + level
    flux_x = depth * ubar
    flux_low = (edges[0][0] + edges[1][0]) * edges[10][0]
    flux_high = (edges[0][1] + edges[1][1]) * edges[10][1]
    flux_y = depth * vbar
    divergence = (
        up(flux_x, flux_high)
        - down(flux_x, flux_low)
        + right(flux_y, plane_count + 3)
        - left(flux_y, plane_count + 3)
    )
    level_ref[...] = level - 0.5 * LAM_O * wet * divergence
    inverse = 1.0 / depth
    grad_x = 0.5 * (up(level, edges[0][1]) - down(level, edges[0][0]))
    grad_y = 0.5 * (right(level, plane_count) - left(level, plane_count))
    xx_x = up(sxx, edges[3][1]) - down(sxx, edges[3][0])
    xy_x = up(sxy, edges[4][1]) - down(sxy, edges[4][0])
    xy_y = right(sxy, plane_count + 1) - left(sxy, plane_count + 1)
    yy_y = right(syy, plane_count + 2) - left(syy, plane_count + 2)
    base = (
        -LAM_O * grad_x - 0.5 * LAM_O * (xx_x + xy_y) * inverse,
        -LAM_O * grad_y - 0.5 * LAM_O * (xy_x + yy_y) * inverse,
    )
    turn = (F_CORIOLIS, -F_CORIOLIS)
    for k in range(levels):
        for c in range(2):
            plane = c * levels + k
            here = vel_ref[c, k]
            other = vel_ref[1 - c, k]
            above = vel_ref[c, max(k - 1, 0)]
            below = vel_ref[c, min(k + 1, levels - 1)]
            block, place = FIELDS + plane // 8, plane % 8
            low = low_ref[block, place : place + 1, :]
            high = high_ref[block, place : place + 1, :]
            around = up(here, high) + down(here, low) + right(here, plane) + left(here, plane)
            tendency = (
                base[c]
                + turn[c] * other
                + NU_H * (around - 4.0 * here)
                + KAPPA_V * (above + below - 2.0 * here)
            )
            out_ref[c, k] = wet * (here + tendency)


def ocean_step(place, vel, *operands):
    return pl.pallas_call(
        ocean_kernel,
        out_shape=(
            jax.ShapeDtypeStruct(vel.shape, F32),
            jax.ShapeDtypeStruct((32, 128), F32),
        ),
        in_specs=[pl.BlockSpec(memory_space=SMEM)] + [pl.BlockSpec(memory_space=VMEM)] * 5,
        out_specs=(pl.BlockSpec(memory_space=VMEM),) * 2,
        compiler_params=params(16),
        cost_estimate=pl.CostEstimate(flops=10000000, bytes_accessed=3000000, transcendentals=0),
        name="ocean_step",
    )(place, vel, *operands)


def shifted(array, axis_name, up):
    count = lax.axis_size(axis_name)
    pairs = [(i, i + 1) for i in range(count - 1)]
    if not up:
        pairs = [(target, source) for source, target in pairs]
    return lax.ppermute(array, axis_name, pairs)


def after(value, *others):
    return lax.optimization_barrier((value,) + others)[0]


def per_device(ocean_level, ocean_velocity, bathymetry, sea_mask, stress_in, spectra, wind_field):
    both = ("wide", "deep")
    spec = spectra.reshape(ND, NF, 2, 4, 128).transpose(0, 1, 3, 2, 4).reshape(ND, NF * 8, 128)
    wind = wind_field.reshape(2, 2, 4, 128).transpose(0, 2, 1, 3).reshape(16, 128)
    trig = jnp.asarray(TRIG)

    own, low_edge, high_edge, first, last = gather_surface(
        ocean_level, ocean_velocity, bathymetry, sea_mask, stress_in
    )
    from_low = shifted(high_edge, "wide", True)
    from_high = shifted(low_edge, "wide", False)
    upper, lower = split_rows(after(spec, own), wind)
    place = lax.axis_index("deep").astype(jnp.int32).reshape(1)
    outgoing = surface_step(place, after(own, upper), from_low, from_high, first, last)
    arrived = lax.all_to_all(outgoing, "deep", split_axis=0, concat_axis=0, tiled=True)

    above = shifted(after(upper, from_low, from_high), both, True)
    below = shifted(after(lower, from_low, from_high), both, False)
    far_above = shifted(after(lower, arrived), both, True)
    far_below = shifted(after(upper, arrived), both, False)
    velocity_out, level_out = ocean_step(
        place, ocean_velocity, own, from_low, from_high, arrived
    )
    begun = begin_step(trig, upper, lower, arrived)
    partial = first_step(
        trig, upper, lower, above, below, *begun, after(arrived, level_out), wind
    )
    spec, stress = second_step(trig, far_above, far_below, *partial)
    stress = lax.all_to_all(stress, "deep", split_axis=0, concat_axis=0, tiled=True)
    stress = stress.reshape(8, 3, 2, 128).transpose(1, 0, 2, 3).reshape(3, 16, 128)
    stress_out = jnp.where((place[0] & 1) == 1, stress[:, :, 64:], stress[:, :, :64])
    spectra_out = (
        spec.reshape(ND, NF, 4, 2, 128).transpose(0, 1, 3, 2, 4).reshape(ND, NF, 2, 512)
    )
    return (level_out, velocity_out, spectra_out, stress_out)


def solution(mesh):
    in_specs = (
        P("wide", "deep"),
        P(None, None, "wide", "deep"),
        P("wide", "deep"),
        P("wide", "deep"),
        P(None, "wide", "deep"),
        P(None, None, ("wide", "deep"), None),
        P(None, ("wide", "deep"), None),
    )
    out_specs = (
        P("wide", "deep"),
        P(None, None, "wide", "deep"),
        P(None, None, ("wide", "deep"), None),
        P(None, "wide", "deep"),
    )
    return jax.shard_map(
        per_device, mesh=mesh, in_specs=in_specs, out_specs=out_specs, check_vma=False
    )
```

profile of v0, /device:TPU:4, one launch (start us, length us, event | category | flops | bytes accessed | tf_op | source)
XLA Modules:
  0.0 120.3 jit_solution(5555288774559776999)
XLA Ops:
  0.6 3.4 %gather_surface.1 = (f32[12,32,128]{2,1,0:T(8,128)}, f32[22,8,128]{2,1,0:T(8,128)}, f32[22,8,128]{2,1,0:T(8,128)}, f32[32,128]{1,0:T(8,128)}, f32[32,128]{1,0:T(8,128)}) custom-call(f32[32,128]{1,0:T(8,128)} %level_ref.1, f32[2,40,32,128]{3,2,1,0:T(8,128)} %vel_ref.3, f32[32,128]{1,0:T(8,128)} %bathy_ref.1, s32[32,128]{1,0:T(8,128)} %mask_ref.1, ...), custom_call_target="tpu_custom_call" | custom-call | flops 400000 | bytes 1700000 | tf_op jit(solution)/shard_map/gather_surface/pallas_call | solution.py:242
  4.0 1.9 %collective-permute-start = (f32[22,8,128]{2,1,0:T(8,128)}, f32[22,8,128]{2,1,0:T(8,128)S(1)}, u32[]{:S(2)}, u32[]{:S(2)}) collective-permute-start(f32[22,8,128]{2,1,0:T(8,128)} %get-tuple-element.34), channel_id=1, source_target_pairs={{0,8},{8,16},{16,24},{24,32},{32,40},{40,48},{48,56},{56,64},{64,7... | collective-permute-start | bytes 270344 | tf_op jit(solution)/shard_map/ppermute | solution.py:995
  6.0 4.5 %collective-permute-start.1 = (f32[22,8,128]{2,1,0:T(8,128)}, f32[22,8,128]{2,1,0:T(8,128)S(1)}, u32[]{:S(2)}, u32[]{:S(2)}) collective-permute-start(f32[22,8,128]{2,1,0:T(8,128)} %get-tuple-element.35), channel_id=1, source_target_pairs={{8,0},{16,8},{24,16},{32,24},{40,32},{48,40},{56,48},{64,56},{72,6... | collective-permute-start | bytes 270344 | tf_op jit(solution)/shard_map/ppermute | solution.py:995
  10.5 0.0 copy-start.3
  10.5 0.0 copy-start.5
  10.5 0.0 copy-start.6
  10.6 4.0 %split_rows.1 = (bf16[5200,128]{1,0:T(8,128)(2,1)}, bf16[5200,128]{1,0:T(8,128)(2,1)}) custom-call(bf16[36,288,128]{2,1,0:T(8,128)(2,1)} %bitcast.22, bf16[16,128]{1,0:T(8,128)(2,1)} %bitcast.20), custom_call_target="tpu_custom_call" | custom-call | flops 4000000 | bytes 9000000 | tf_op jit(solution)/shard_map/split_rows/pallas_call | solution.py:150
  14.5 0.0 collective-permute-done.low_ref
  14.5 0.0 collective-permute-done.1.high_ref
  14.6 0.0 copy-start.7
  14.6 0.0 copy-start.1
  14.6 1.4 %surface_step.1 = f32[8,72,128]{2,1,0:T(8,128)} custom-call(s32[1]{0:T(128)} %bitcast.place_ref, f32[12,32,128]{2,1,0:T(8,128)S(1)} %copy-done.3, f32[22,8,128]{2,1,0:T(8,128)S(1)} %collective-permute-done.low_ref, f32[22,8,128]{2,1,0:T(8,128)S(1)} %collective-permute-done.1.high_ref, f32[32,128]{1,0:T(8,128)S(1)} %copy-done.5, f32[32,128]{1,0:T(8,128)S(1)} %copy-done.6), custom_call_target="tpu_custom_call" | custom-call | flops 2000000 | bytes 400000 | tf_op jit(solution)/shard_map/surface_step/pallas_call | solution.py:365
  16.0 7.9 %all-to-all-start = ((f32[8,72,128]{2,1,0:T(8,128)}), f32[8,72,128]{2,1,0:T(8,128)S(1)}, u32[]{:S(2)}, u32[]{:S(2)}) async-start(f32[8,72,128]{2,1,0:T(8,128)} %surface_step.1), calls=%async_computation | async-start | bytes 589824 | tf_op jit(solution)/shard_map/all_to_all | solution.py:1016
  23.9 3.9 %collective-permute-start.4 = (bf16[5200,128]{1,0:T(8,128)(2,1)}, bf16[5200,128]{1,0:T(8,128)(2,1)}, u32[]{:S(2)}, u32[]{:S(2)}) collective-permute-start(bf16[5200,128]{1,0:T(8,128)(2,1)} %get-tuple-element.46.upper_ref), channel_id=1, source_target_pairs={{0,1},{1,2},{2,3},{3,4},{4,5},{5,6},{6,7},{7,8},{8,9},{9,10},{10,1... | collective-permute-start | bytes 3993608 | tf_op jit(solution)/shard_map/ppermute | solution.py:995
  27.9 5.9 %collective-permute-start.5 = (bf16[5200,128]{1,0:T(8,128)(2,1)}, bf16[5200,128]{1,0:T(8,128)(2,1)}, u32[]{:S(2)}, u32[]{:S(2)}) collective-permute-start(bf16[5200,128]{1,0:T(8,128)(2,1)} %get-tuple-element.47.lower_ref), channel_id=1, source_target_pairs={{1,0},{2,1},{3,2},{4,3},{5,4},{6,5},{7,6},{8,7},{9,8},{10,9},{11,1... | collective-permute-start | bytes 3993608 | tf_op jit(solution)/shard_map/ppermute | solution.py:995
  33.7 0.2 all-to-all-done.arrived_ref
  33.9 1.9 %collective-permute-start.3 = (bf16[5200,128]{1,0:T(8,128)(2,1)}, bf16[5200,128]{1,0:T(8,128)(2,1)S(1)}, u32[]{:S(2)}, u32[]{:S(2)}) collective-permute-start(bf16[5200,128]{1,0:T(8,128)(2,1)} %get-tuple-element.46.upper_ref), channel_id=1, source_target_pairs={{1,0},{2,1},{3,2},{4,3},{5,4},{6,5},{7,6},{8,7},{9,8},{10,9},{11,1... | collective-permute-start | bytes 3993608 | tf_op jit(solution)/shard_map/ppermute | solution.py:995
  35.8 3.9 %collective-permute-start.2 = (bf16[5200,128]{1,0:T(8,128)(2,1)}, bf16[5200,128]{1,0:T(8,128)(2,1)S(1)}, u32[]{:S(2)}, u32[]{:S(2)}) collective-permute-start(bf16[5200,128]{1,0:T(8,128)(2,1)} %get-tuple-element.47.lower_ref), channel_id=1, source_target_pairs={{0,1},{1,2},{2,3},{3,4},{4,5},{5,6},{6,7},{7,8},{8,9},{9,10},{10,1... | collective-permute-start | bytes 3993608 | tf_op jit(solution)/shard_map/ppermute | solution.py:995
  39.8 0.0 copy-start.2
  39.8 1.3 %copy-done.2 = f32[2,40,32,128]{3,2,1,0:T(8,128)S(1)} copy-done((f32[2,40,32,128]{3,2,1,0:T(8,128)S(1)}, f32[2,40,32,128]{3,2,1,0:T(8,128)}, u32[]{:S(2)}) %copy-start.2) | copy-done | bytes 1310744
  41.1 2.9 %ocean_step.1 = (f32[2,40,32,128]{3,2,1,0:T(8,128)}, f32[32,128]{1,0:T(8,128)}) custom-call(s32[1]{0:T(128)} %bitcast.place_ref, f32[2,40,32,128]{3,2,1,0:T(8,128)S(1)} %copy-done.2, f32[12,32,128]{2,1,0:T(8,128)S(1)} %copy-done.3, f32[22,8,128]{2,1,0:T(8,128)S(1)} %collective-permute-done.low_ref, f32[22,8,128]{2,1,0:T(8,128)S(1)} %collective-permute-done.1.high_ref, ...), custom_call_target="tpu_custom_call" | custom-call | flops 10000000 | bytes 3000000 | tf_op jit(solution)/shard_map/ocean_step/pallas_call | solution.py:976
  44.0 0.0 copy-start.4
  44.0 7.7 %begin_wave_step.1 = (bf16[5184,128]{1,0:T(8,128)(2,1)S(1)}, bf16[5184,128]{1,0:T(8,128)(2,1)S(1)}) custom-call(f32[2,36]{1,0:T(2,128)S(1)} %copy-done.7, bf16[5200,128]{1,0:T(8,128)(2,1)S(1)} %copy-done.1, bf16[5200,128]{1,0:T(8,128)(2,1)S(1)} %copy-done, f32[8,72,128]{2,1,0:T(8,128)S(1)} %all-to-all-done.arrived_ref), custom_call_target="tpu_custom_call" | custom-call | flops 100000000 | bytes 20000000 | tf_op jit(solution)/shard_map/begin_wave_step/pallas_call | solution.py:632
  51.7 6.5 %collective-permute-done.4.above_ref = bf16[5200,128]{1,0:T(8,128)(2,1)} collective-permute-done((bf16[5200,128]{1,0:T(8,128)(2,1)}, bf16[5200,128]{1,0:T(8,128)(2,1)}, u32[]{:S(2)}, u32[]{:S(2)}) %collective-permute-start.4) | collective-permute-done | bytes 1331232 | tf_op jit(solution)/shard_map/ppermute | solution.py:995
  58.1 4.1 %collective-permute-done.5.below_ref = bf16[5200,128]{1,0:T(8,128)(2,1)} collective-permute-done((bf16[5200,128]{1,0:T(8,128)(2,1)}, bf16[5200,128]{1,0:T(8,128)(2,1)}, u32[]{:S(2)}, u32[]{:S(2)}) %collective-permute-start.5) | collective-permute-done | bytes 1331232 | tf_op jit(solution)/shard_map/ppermute | solution.py:995
  62.2 21.5 %first_wave_step.1 = (bf16[5184,128]{1,0:T(8,128)(2,1)S(1)}, bf16[5184,128]{1,0:T(8,128)(2,1)S(1)}, bf16[5184,128]{1,0:T(8,128)(2,1)S(1)}, bf16[5184,128]{1,0:T(...) custom-call(f32[2,36]{1,0:T(2,128)S(1)} %copy-done.7, ...), custom_call_target="tpu_custom_call" | custom-call | flops 100000000 | bytes 60000000 | tf_op jit(solution)/shard_map/first_wave_step/pallas_call | solution.py:861
  83.7 4.3 %collective-permute-done.3.far_below_ref = bf16[5200,128]{1,0:T(8,128)(2,1)S(1)} collective-permute-done((bf16[5200,128]{1,0:T(8,128)(2,1)}, bf16[5200,128]{1,0:T(8,128)(2,1)S(1)}, u32[]{:S(2)}, u32[]{:S(2)}) %collective-permute-start.3) | collective-permute-done | bytes 1331232 | tf_op jit(solution)/shard_map/ppermute | solution.py:995
  87.9 0.0 collective-permute-done.2.far_above_ref
  88.0 11.2 %second_wave_step.1 = (bf16[36,288,128]{2,1,0:T(8,128)(2,1)}, f32[8,6,128]{2,1,0:T(8,128)}) custom-call(f32[2,36]{1,0:T(2,128)S(1)} %copy-done.7, bf16[5200,128]{1,0:T(8,128)(2,1)S(1)} %collective-permute-done.2.far_above_ref, bf16[5200,128]{1,0:T(8,128)(2,1)S(1)} %collective-permute-done.3.far_below_ref, ...), custom_call_target="tpu_custom_call" | custom-call | flops 200000000 | bytes 40000000 | tf_op jit(solution)/shard_map/second_wave_step/pallas_call | solution.py:879
  99.2 12.6 %all-to-all-start.1 = ((f32[8,6,128]{2,1,0:T(8,128)}), f32[8,6,128]{2,1,0:T(8,128)S(1)}, u32[]{:S(2)}, u32[]{:S(2)}) async-start(f32[8,6,128]{2,1,0:T(8,128)} %get-tuple-element.61), calls=%async_computation.1 | async-start | bytes 65536 | tf_op jit(solution)/shard_map/all_to_all | solution.py:1030
  111.8 7.8 %all-to-all-done.1 = f32[8,6,128]{2,1,0:T(8,128)S(1)} async-done(((f32[8,6,128]{2,1,0:T(8,128)}), f32[8,6,128]{2,1,0:T(8,128)S(1)}, u32[]{:S(2)}, u32[]{:S(2)}) %all-to-all-start.1) | async-done | bytes 24608 | tf_op jit(solution)/shard_map/all_to_all | solution.py:1030
  119.6 0.7 slice_select_fusion
  (10 shorter events, 0.0 us)
Async XLA Ops:
  4.0 10.5 %collective-permute-start = (f32[22,8,128]{2,1,0:T(8,128)}, f32[22,8,128]{2,1,0:T(8,128)S(1)}, u32[]{:S(2)}, u32[]{:S(2)}) collective-permute-start(f32[22,8,128]{2,1,0:T(8,128)} %get-tuple-element.34), channel_id=1, source_target_pairs={{0,8},{8,16},{16,24},{24,32},{32,40},{40,48},{48,56},{56,64},{64,7... | collective-permute-start | bytes 270344 | tf_op jit(solution)/shard_map/ppermute | solution.py:995
  6.0 8.6 %collective-permute-start.1 = (f32[22,8,128]{2,1,0:T(8,128)}, f32[22,8,128]{2,1,0:T(8,128)S(1)}, u32[]{:S(2)}, u32[]{:S(2)}) collective-permute-start(f32[22,8,128]{2,1,0:T(8,128)} %get-tuple-element.35), channel_id=1, source_target_pairs={{8,0},{16,8},{24,16},{32,24},{40,32},{48,40},{56,48},{64,56},{72,6... | collective-permute-start | bytes 270344 | tf_op jit(solution)/shard_map/ppermute | solution.py:995
  10.5 4.0 %copy-start.3 = (f32[12,32,128]{2,1,0:T(8,128)S(1)}, f32[12,32,128]{2,1,0:T(8,128)}, u32[]{:S(2)}) copy-start(f32[12,32,128]{2,1,0:T(8,128)} %get-tuple-element.38.own_ref) | copy-start | bytes 589828
  10.5 4.0 %copy-start.5 = (f32[32,128]{1,0:T(8,128)S(1)}, f32[32,128]{1,0:T(8,128)}, u32[]{:S(2)}) copy-start(f32[32,128]{1,0:T(8,128)} %get-tuple-element.39.first_ref) | copy-start | bytes 49156
  10.5 4.0 %copy-start.6 = (f32[32,128]{1,0:T(8,128)S(1)}, f32[32,128]{1,0:T(8,128)}, u32[]{:S(2)}) copy-start(f32[32,128]{1,0:T(8,128)} %get-tuple-element.40.last_ref) | copy-start | bytes 49156
  14.6 29.4 %copy-start.7 = (f32[2,36]{1,0:T(2,128)S(1)}, f32[2,36]{1,0:T(2,128)}, u32[]{:S(2)}) copy-start(f32[2,36]{1,0:T(2,128)} %constant.8.clone.trig_ref) | copy-start | bytes 868
  14.6 29.4 %copy-start.1 = (bf16[5200,128]{1,0:T(8,128)(2,1)S(1)}, bf16[5200,128]{1,0:T(8,128)(2,1)}, u32[]{:S(2)}) copy-start(bf16[5200,128]{1,0:T(8,128)(2,1)} %get-tuple-element.46.upper_ref) | copy-start | bytes 3993604
  16.0 28.0 %copy-start = (bf16[5200,128]{1,0:T(8,128)(2,1)S(1)}, bf16[5200,128]{1,0:T(8,128)(2,1)}, u32[]{:S(2)}) copy-start(bf16[5200,128]{1,0:T(8,128)(2,1)} %get-tuple-element.47.lower_ref) | copy-start | bytes 3993604
  16.0 17.9 %all-to-all-start = ((f32[8,72,128]{2,1,0:T(8,128)}), f32[8,72,128]{2,1,0:T(8,128)S(1)}, u32[]{:S(2)}, u32[]{:S(2)}) async-start(f32[8,72,128]{2,1,0:T(8,128)} %surface_step.1), calls=%async_computation | async-start | bytes 589824 | tf_op jit(solution)/shard_map/all_to_all | solution.py:1016
  23.9 34.2 %collective-permute-start.4 = (bf16[5200,128]{1,0:T(8,128)(2,1)}, bf16[5200,128]{1,0:T(8,128)(2,1)}, u32[]{:S(2)}, u32[]{:S(2)}) collective-permute-start(bf16[5200,128]{1,0:T(8,128)(2,1)} %get-tuple-element.46.upper_ref), channel_id=1, source_target_pairs={{0,1},{1,2},{2,3},{3,4},{4,5},{5,6},{6,7},{7,8},{8,9},{9,10},{10,1... | collective-permute-start | bytes 3993608 | tf_op jit(solution)/shard_map/ppermute | solution.py:995
  27.9 34.4 %collective-permute-start.5 = (bf16[5200,128]{1,0:T(8,128)(2,1)}, bf16[5200,128]{1,0:T(8,128)(2,1)}, u32[]{:S(2)}, u32[]{:S(2)}) collective-permute-start(bf16[5200,128]{1,0:T(8,128)(2,1)} %get-tuple-element.47.lower_ref), channel_id=1, source_target_pairs={{1,0},{2,1},{3,2},{4,3},{5,4},{6,5},{7,6},{8,7},{9,8},{10,9},{11,1... | collective-permute-start | bytes 3993608 | tf_op jit(solution)/shard_map/ppermute | solution.py:995
  33.9 54.0 %collective-permute-start.3 = (bf16[5200,128]{1,0:T(8,128)(2,1)}, bf16[5200,128]{1,0:T(8,128)(2,1)S(1)}, u32[]{:S(2)}, u32[]{:S(2)}) collective-permute-start(bf16[5200,128]{1,0:T(8,128)(2,1)} %get-tuple-element.46.upper_ref), channel_id=1, source_target_pairs={{1,0},{2,1},{3,2},{4,3},{5,4},{6,5},{7,6},{8,7},{9,8},{10,9},{11,1... | collective-permute-start | bytes 3993608 | tf_op jit(solution)/shard_map/ppermute | solution.py:995
  35.8 52.1 %collective-permute-start.2 = (bf16[5200,128]{1,0:T(8,128)(2,1)}, bf16[5200,128]{1,0:T(8,128)(2,1)S(1)}, u32[]{:S(2)}, u32[]{:S(2)}) collective-permute-start(bf16[5200,128]{1,0:T(8,128)(2,1)} %get-tuple-element.47.lower_ref), channel_id=1, source_target_pairs={{0,1},{1,2},{2,3},{3,4},{4,5},{5,6},{6,7},{7,8},{8,9},{9,10},{10,1... | collective-permute-start | bytes 3993608 | tf_op jit(solution)/shard_map/ppermute | solution.py:995
  39.8 1.3 %copy-start.2 = (f32[2,40,32,128]{3,2,1,0:T(8,128)S(1)}, f32[2,40,32,128]{3,2,1,0:T(8,128)}, u32[]{:S(2)}) copy-start(f32[2,40,32,128]{3,2,1,0:T(8,128)} %vel_ref.3) | copy-start | bytes 3932164
  44.0 18.3 %copy-start.4 = (bf16[2,2,512]{2,1,0:T(2,128)(2,1)S(1)}, bf16[2,2,512]{2,1,0:T(2,128)(2,1)}, u32[]{:S(2)}) copy-start(bf16[2,2,512]{2,1,0:T(2,128)(2,1)} %param.14) | copy-start | bytes 12292
  99.2 20.4 %all-to-all-start.1 = ((f32[8,6,128]{2,1,0:T(8,128)}), f32[8,6,128]{2,1,0:T(8,128)S(1)}, u32[]{:S(2)}, u32[]{:S(2)}) async-start(f32[8,6,128]{2,1,0:T(8,128)} %get-tuple-element.61), calls=%async_computation.1 | async-start | bytes 65536 | tf_op jit(solution)/shard_map/all_to_all | solution.py:1030
where the time goes:
time: 121 us; the launch traced here: 120 us
  Pallas kernels  52 us (43%)
  starting transfers between devices  42.6 us (35%)
  waiting for transfers between devices  22.8 us (19%)
  local copies, waits for them, and re-layouts  1.38 us (1%)
    ppermute x6, starting transfers between devices, shifted(): return lax.ppermute(array, axis_name, pairs)  22.1 us
    pallas_call x1, Pallas kernels, first_step(): pl.pallas_call(first_kernel, out_shape=(jax.ShapeDtypeStruct((HALF_ROWS,...  21.5 us
    ppermute x6, waiting for transfers between devices, shifted(): return lax.ppermute(array, axis_name, pairs)  14.8 us
    all_to_all x1, starting transfers between devices, per_device(): lax.all_to_all(stress, 'deep', split_axis=0, concat_axis=0, tiled=True)  12.6 us
    pallas_call x1, Pallas kernels, second_step(): pl.pallas_call(second_kernel, out_shape=(full, jax.ShapeDtypeStruct((8, 6...  11.2 us
    all_to_all x1, starting transfers between devices, per_device(): lax.all_to_all(outgoing, 'deep', split_axis=0, concat_axis=0, tiled=True)  7.91 us
    all_to_all x1, waiting for transfers between devices, per_device(): lax.all_to_all(stress, 'deep', split_axis=0, concat_axis=0, tiled=True)  7.76 us
    pallas_call x1, Pallas kernels, begin_step(): pl.pallas_call(begin_kernel, out_shape=(jax.ShapeDtypeStruct((HALF_ROWS,...  7.65 us
  transfers between devices with their start and end apart: 8, of which 5 were waited for; matrix products, arithmetic and copies ran while one was open for 0% of the time, Pallas kernels for 30%

commit v1 on v0

--- a/solution.py
+++ b/solution.py
@@ -39,7 +39,7 @@
 BINS = ND * NF
 CELL_ROWS = BINS * 8
 PAD = 16
-CHUNK = 6
+CHUNK = 3
 
 
 def iotas():

time: 121 us -> 121 us (level)
  no operation moved by 1% of the time
where the time goes in v1:
time: 121 us; the launch traced here: 120 us
  Pallas kernels  52 us (43%)
  starting transfers between devices  42.6 us (35%)
  waiting for transfers between devices  22.8 us (19%)
  local copies, waits for them, and re-layouts  1.38 us (1%)
    ppermute x6, starting transfers between devices, shifted(): return lax.ppermute(array, axis_name, pairs)  22.1 us
    pallas_call x1, Pallas kernels, first_step(): pl.pallas_call(first_kernel, out_shape=(jax.ShapeDtypeStruct((HALF_ROWS,...  21.5 us
    ppermute x6, waiting for transfers between devices, shifted(): return lax.ppermute(array, axis_name, pairs)  14.8 us
    all_to_all x1, starting transfers between devices, per_device(): lax.all_to_all(stress, 'deep', split_axis=0, concat_axis=0, tiled=True)  12.6 us
    pallas_call x1, Pallas kernels, second_step(): pl.pallas_call(second_kernel, out_shape=(full, jax.ShapeDtypeStruct((8, 6...  11.2 us
    all_to_all x1, starting transfers between devices, per_device(): lax.all_to_all(outgoing, 'deep', split_axis=0, concat_axis=0, tiled=True)  7.91 us
    all_to_all x1, waiting for transfers between devices, per_device(): lax.all_to_all(stress, 'deep', split_axis=0, concat_axis=0, tiled=True)  7.76 us
    pallas_call x1, Pallas kernels, begin_step(): pl.pallas_call(begin_kernel, out_shape=(jax.ShapeDtypeStruct((HALF_ROWS,...  7.65 us
  transfers between devices with their start and end apart: 8, of which 5 were waited for; matrix products, arithmetic and copies ran while one was open for 0% of the time, Pallas kernels for 30%

profile of v1, /device:TPU:4, one launch (start us, length us, event | category | flops | bytes accessed | tf_op | source)
XLA Modules:
  0.0 120.3 jit_solution(2101147326096260234)
XLA Ops:
  0.6 3.4 %gather_surface.1 = (f32[12,32,128]{2,1,0:T(8,128)}, f32[22,8,128]{2,1,0:T(8,128)}, f32[22,8,128]{2,1,0:T(8,128)}, f32[32,128]{1,0:T(8,128)}, f32[32,128]{1,0:T(8,128)}) custom-call(f32[32,128]{1,0:T(8,128)} %level_ref.1, f32[2,40,32,128]{3,2,1,0:T(8,128)} %vel_ref.3, f32[32,128]{1,0:T(8,128)} %bathy_ref.1, s32[32,128]{1,0:T(8,128)} %mask_ref.1, ...), custom_call_target="tpu_custom_call" | custom-call | flops 400000 | bytes 1700000 | tf_op jit(solution)/shard_map/gather_surface/pallas_call | solution.py:242
  4.0 1.9 %collective-permute-start = (f32[22,8,128]{2,1,0:T(8,128)}, f32[22,8,128]{2,1,0:T(8,128)S(1)}, u32[]{:S(2)}, u32[]{:S(2)}) collective-permute-start(f32[22,8,128]{2,1,0:T(8,128)} %get-tuple-element.34), channel_id=1, source_target_pairs={{0,8},{8,16},{16,24},{24,32},{32,40},{40,48},{48,56},{56,64},{64,7... | collective-permute-start | bytes 270344 | tf_op jit(solution)/shard_map/ppermute | solution.py:995
  6.0 4.5 %collective-permute-start.1 = (f32[22,8,128]{2,1,0:T(8,128)}, f32[22,8,128]{2,1,0:T(8,128)S(1)}, u32[]{:S(2)}, u32[]{:S(2)}) collective-permute-start(f32[22,8,128]{2,1,0:T(8,128)} %get-tuple-element.35), channel_id=1, source_target_pairs={{8,0},{16,8},{24,16},{32,24},{40,32},{48,40},{56,48},{64,56},{72,6... | collective-permute-start | bytes 270344 | tf_op jit(solution)/shard_map/ppermute | solution.py:995
  10.5 0.0 copy-start.3
  10.5 0.0 copy-start.5
  10.5 0.0 copy-start.6
  10.6 4.0 %split_rows.1 = (bf16[5200,128]{1,0:T(8,128)(2,1)}, bf16[5200,128]{1,0:T(8,128)(2,1)}) custom-call(bf16[36,288,128]{2,1,0:T(8,128)(2,1)} %bitcast.22, bf16[16,128]{1,0:T(8,128)(2,1)} %bitcast.20), custom_call_target="tpu_custom_call" | custom-call | flops 4000000 | bytes 9000000 | tf_op jit(solution)/shard_map/split_rows/pallas_call | solution.py:150
  14.5 0.0 collective-permute-done.low_ref
  14.6 0.0 collective-permute-done.1.high_ref
  14.6 0.0 copy-start.7
  14.6 0.0 copy-start.1
  14.6 1.4 %surface_step.1 = f32[8,72,128]{2,1,0:T(8,128)} custom-call(s32[1]{0:T(128)} %bitcast.place_ref, f32[12,32,128]{2,1,0:T(8,128)S(1)} %copy-done.3, f32[22,8,128]{2,1,0:T(8,128)S(1)} %collective-permute-done.low_ref, f32[22,8,128]{2,1,0:T(8,128)S(1)} %collective-permute-done.1.high_ref, f32[32,128]{1,0:T(8,128)S(1)} %copy-done.5, f32[32,128]{1,0:T(8,128)S(1)} %copy-done.6), custom_call_target="tpu_custom_call" | custom-call | flops 2000000 | bytes 400000 | tf_op jit(solution)/shard_map/surface_step/pallas_call | solution.py:365
  16.0 7.9 %all-to-all-start = ((f32[8,72,128]{2,1,0:T(8,128)}), f32[8,72,128]{2,1,0:T(8,128)S(1)}, u32[]{:S(2)}, u32[]{:S(2)}) async-start(f32[8,72,128]{2,1,0:T(8,128)} %surface_step.1), calls=%async_computation | async-start | bytes 589824 | tf_op jit(solution)/shard_map/all_to_all | solution.py:1016
  24.0 3.9 %collective-permute-start.4 = (bf16[5200,128]{1,0:T(8,128)(2,1)}, bf16[5200,128]{1,0:T(8,128)(2,1)}, u32[]{:S(2)}, u32[]{:S(2)}) collective-permute-start(bf16[5200,128]{1,0:T(8,128)(2,1)} %get-tuple-element.46.upper_ref), channel_id=1, source_target_pairs={{0,1},{1,2},{2,3},{3,4},{4,5},{5,6},{6,7},{7,8},{8,9},{9,10},{10,1... | collective-permute-start | bytes 3993608 | tf_op jit(solution)/shard_map/ppermute | solution.py:995
  27.9 5.9 %collective-permute-start.5 = (bf16[5200,128]{1,0:T(8,128)(2,1)}, bf16[5200,128]{1,0:T(8,128)(2,1)}, u32[]{:S(2)}, u32[]{:S(2)}) collective-permute-start(bf16[5200,128]{1,0:T(8,128)(2,1)} %get-tuple-element.47.lower_ref), channel_id=1, source_target_pairs={{1,0},{2,1},{3,2},{4,3},{5,4},{6,5},{7,6},{8,7},{9,8},{10,9},{11,1... | collective-permute-start | bytes 3993608 | tf_op jit(solution)/shard_map/ppermute | solution.py:995
  33.7 0.2 all-to-all-done.arrived_ref
  33.9 1.9 %collective-permute-start.3 = (bf16[5200,128]{1,0:T(8,128)(2,1)}, bf16[5200,128]{1,0:T(8,128)(2,1)S(1)}, u32[]{:S(2)}, u32[]{:S(2)}) collective-permute-start(bf16[5200,128]{1,0:T(8,128)(2,1)} %get-tuple-element.46.upper_ref), channel_id=1, source_target_pairs={{1,0},{2,1},{3,2},{4,3},{5,4},{6,5},{7,6},{8,7},{9,8},{10,9},{11,1... | collective-permute-start | bytes 3993608 | tf_op jit(solution)/shard_map/ppermute | solution.py:995
  35.8 3.9 %collective-permute-start.2 = (bf16[5200,128]{1,0:T(8,128)(2,1)}, bf16[5200,128]{1,0:T(8,128)(2,1)S(1)}, u32[]{:S(2)}, u32[]{:S(2)}) collective-permute-start(bf16[5200,128]{1,0:T(8,128)(2,1)} %get-tuple-element.47.lower_ref), channel_id=1, source_target_pairs={{0,1},{1,2},{2,3},{3,4},{4,5},{5,6},{6,7},{7,8},{8,9},{9,10},{10,1... | collective-permute-start | bytes 3993608 | tf_op jit(solution)/shard_map/ppermute | solution.py:995
  39.8 0.0 copy-start.2
  39.8 1.3 %copy-done.2 = f32[2,40,32,128]{3,2,1,0:T(8,128)S(1)} copy-done((f32[2,40,32,128]{3,2,1,0:T(8,128)S(1)}, f32[2,40,32,128]{3,2,1,0:T(8,128)}, u32[]{:S(2)}) %copy-start.2) | copy-done | bytes 1310744
  41.1 2.9 %ocean_step.1 = (f32[2,40,32,128]{3,2,1,0:T(8,128)}, f32[32,128]{1,0:T(8,128)}) custom-call(s32[1]{0:T(128)} %bitcast.place_ref, f32[2,40,32,128]{3,2,1,0:T(8,128)S(1)} %copy-done.2, f32[12,32,128]{2,1,0:T(8,128)S(1)} %copy-done.3, f32[22,8,128]{2,1,0:T(8,128)S(1)} %collective-permute-done.low_ref, f32[22,8,128]{2,1,0:T(8,128)S(1)} %collective-permute-done.1.high_ref, ...), custom_call_target="tpu_custom_call" | custom-call | flops 10000000 | bytes 3000000 | tf_op jit(solution)/shard_map/ocean_step/pallas_call | solution.py:976
  44.0 0.0 copy-start.4
  44.0 7.7 %begin_wave_step.1 = (bf16[5184,128]{1,0:T(8,128)(2,1)S(1)}, bf16[5184,128]{1,0:T(8,128)(2,1)S(1)}) custom-call(f32[2,36]{1,0:T(2,128)S(1)} %copy-done.7, bf16[5200,128]{1,0:T(8,128)(2,1)S(1)} %copy-done.1, bf16[5200,128]{1,0:T(8,128)(2,1)S(1)} %copy-done, f32[8,72,128]{2,1,0:T(8,128)S(1)} %all-to-all-done.arrived_ref), custom_call_target="tpu_custom_call" | custom-call | flops 100000000 | bytes 20000000 | tf_op jit(solution)/shard_map/begin_wave_step/pallas_call | solution.py:632
  51.7 6.4 %collective-permute-done.4.above_ref = bf16[5200,128]{1,0:T(8,128)(2,1)} collective-permute-done((bf16[5200,128]{1,0:T(8,128)(2,1)}, bf16[5200,128]{1,0:T(8,128)(2,1)}, u32[]{:S(2)}, u32[]{:S(2)}) %collective-permute-start.4) | collective-permute-done | bytes 1331232 | tf_op jit(solution)/shard_map/ppermute | solution.py:995
  58.1 4.1 %collective-permute-done.5.below_ref = bf16[5200,128]{1,0:T(8,128)(2,1)} collective-permute-done((bf16[5200,128]{1,0:T(8,128)(2,1)}, bf16[5200,128]{1,0:T(8,128)(2,1)}, u32[]{:S(2)}, u32[]{:S(2)}) %collective-permute-start.5) | collective-permute-done | bytes 1331232 | tf_op jit(solution)/shard_map/ppermute | solution.py:995
  62.2 21.5 %first_wave_step.1 = (bf16[5184,128]{1,0:T(8,128)(2,1)S(1)}, bf16[5184,128]{1,0:T(8,128)(2,1)S(1)}, bf16[5184,128]{1,0:T(8,128)(2,1)S(1)}, bf16[5184,128]{1,0:T(...) custom-call(f32[2,36]{1,0:T(2,128)S(1)} %copy-done.7, ...), custom_call_target="tpu_custom_call" | custom-call | flops 100000000 | bytes 60000000 | tf_op jit(solution)/shard_map/first_wave_step/pallas_call | solution.py:861
  83.7 4.2 %collective-permute-done.3.far_below_ref = bf16[5200,128]{1,0:T(8,128)(2,1)S(1)} collective-permute-done((bf16[5200,128]{1,0:T(8,128)(2,1)}, bf16[5200,128]{1,0:T(8,128)(2,1)S(1)}, u32[]{:S(2)}, u32[]{:S(2)}) %collective-permute-start.3) | collective-permute-done | bytes 1331232 | tf_op jit(solution)/shard_map/ppermute | solution.py:995
  87.9 0.0 collective-permute-done.2.far_above_ref
  88.0 11.2 %second_wave_step.1 = (bf16[36,288,128]{2,1,0:T(8,128)(2,1)}, f32[8,6,128]{2,1,0:T(8,128)}) custom-call(f32[2,36]{1,0:T(2,128)S(1)} %copy-done.7, bf16[5200,128]{1,0:T(8,128)(2,1)S(1)} %collective-permute-done.2.far_above_ref, bf16[5200,128]{1,0:T(8,128)(2,1)S(1)} %collective-permute-done.3.far_below_ref, ...), custom_call_target="tpu_custom_call" | custom-call | flops 200000000 | bytes 40000000 | tf_op jit(solution)/shard_map/second_wave_step/pallas_call | solution.py:879
  99.2 12.6 %all-to-all-start.1 = ((f32[8,6,128]{2,1,0:T(8,128)}), f32[8,6,128]{2,1,0:T(8,128)S(1)}, u32[]{:S(2)}, u32[]{:S(2)}) async-start(f32[8,6,128]{2,1,0:T(8,128)} %get-tuple-element.61), calls=%async_computation.1 | async-start | bytes 65536 | tf_op jit(solution)/shard_map/all_to_all | solution.py:1030
  111.8 7.8 %all-to-all-done.1 = f32[8,6,128]{2,1,0:T(8,128)S(1)} async-done(((f32[8,6,128]{2,1,0:T(8,128)}), f32[8,6,128]{2,1,0:T(8,128)S(1)}, u32[]{:S(2)}, u32[]{:S(2)}) %all-to-all-start.1) | async-done | bytes 24608 | tf_op jit(solution)/shard_map/all_to_all | solution.py:1030
  119.6 0.7 slice_select_fusion
  (10 shorter events, 0.0 us)
Async XLA Ops:
  4.0 10.5 %collective-permute-start = (f32[22,8,128]{2,1,0:T(8,128)}, f32[22,8,128]{2,1,0:T(8,128)S(1)}, u32[]{:S(2)}, u32[]{:S(2)}) collective-permute-start(f32[22,8,128]{2,1,0:T(8,128)} %get-tuple-element.34), channel_id=1, source_target_pairs={{0,8},{8,16},{16,24},{24,32},{32,40},{40,48},{48,56},{56,64},{64,7... | collective-permute-start | bytes 270344 | tf_op jit(solution)/shard_map/ppermute | solution.py:995
  6.0 8.6 %collective-permute-start.1 = (f32[22,8,128]{2,1,0:T(8,128)}, f32[22,8,128]{2,1,0:T(8,128)S(1)}, u32[]{:S(2)}, u32[]{:S(2)}) collective-permute-start(f32[22,8,128]{2,1,0:T(8,128)} %get-tuple-element.35), channel_id=1, source_target_pairs={{8,0},{16,8},{24,16},{32,24},{40,32},{48,40},{56,48},{64,56},{72,6... | collective-permute-start | bytes 270344 | tf_op jit(solution)/shard_map/ppermute | solution.py:995
  10.5 4.1 %copy-start.3 = (f32[12,32,128]{2,1,0:T(8,128)S(1)}, f32[12,32,128]{2,1,0:T(8,128)}, u32[]{:S(2)}) copy-start(f32[12,32,128]{2,1,0:T(8,128)} %get-tuple-element.38.own_ref) | copy-start | bytes 589828
  10.5 4.1 %copy-start.5 = (f32[32,128]{1,0:T(8,128)S(1)}, f32[32,128]{1,0:T(8,128)}, u32[]{:S(2)}) copy-start(f32[32,128]{1,0:T(8,128)} %get-tuple-element.39.first_ref) | copy-start | bytes 49156
  10.5 4.1 %copy-start.6 = (f32[32,128]{1,0:T(8,128)S(1)}, f32[32,128]{1,0:T(8,128)}, u32[]{:S(2)}) copy-start(f32[32,128]{1,0:T(8,128)} %get-tuple-element.40.last_ref) | copy-start | bytes 49156
  14.6 29.4 %copy-start.7 = (f32[2,36]{1,0:T(2,128)S(1)}, f32[2,36]{1,0:T(2,128)}, u32[]{:S(2)}) copy-start(f32[2,36]{1,0:T(2,128)} %constant.8.clone.trig_ref) | copy-start | bytes 868
  14.6 29.4 %copy-start.1 = (bf16[5200,128]{1,0:T(8,128)(2,1)S(1)}, bf16[5200,128]{1,0:T(8,128)(2,1)}, u32[]{:S(2)}) copy-start(bf16[5200,128]{1,0:T(8,128)(2,1)} %get-tuple-element.46.upper_ref) | copy-start | bytes 3993604
  16.0 28.0 %copy-start = (bf16[5200,128]{1,0:T(8,128)(2,1)S(1)}, bf16[5200,128]{1,0:T(8,128)(2,1)}, u32[]{:S(2)}) copy-start(bf16[5200,128]{1,0:T(8,128)(2,1)} %get-tuple-element.47.lower_ref) | copy-start | bytes 3993604
  16.0 17.9 %all-to-all-start = ((f32[8,72,128]{2,1,0:T(8,128)}), f32[8,72,128]{2,1,0:T(8,128)S(1)}, u32[]{:S(2)}, u32[]{:S(2)}) async-start(f32[8,72,128]{2,1,0:T(8,128)} %surface_step.1), calls=%async_computation | async-start | bytes 589824 | tf_op jit(solution)/shard_map/all_to_all | solution.py:1016
  24.0 34.2 %collective-permute-start.4 = (bf16[5200,128]{1,0:T(8,128)(2,1)}, bf16[5200,128]{1,0:T(8,128)(2,1)}, u32[]{:S(2)}, u32[]{:S(2)}) collective-permute-start(bf16[5200,128]{1,0:T(8,128)(2,1)} %get-tuple-element.46.upper_ref), channel_id=1, source_target_pairs={{0,1},{1,2},{2,3},{3,4},{4,5},{5,6},{6,7},{7,8},{8,9},{9,10},{10,1... | collective-permute-start | bytes 3993608 | tf_op jit(solution)/shard_map/ppermute | solution.py:995
  27.9 34.4 %collective-permute-start.5 = (bf16[5200,128]{1,0:T(8,128)(2,1)}, bf16[5200,128]{1,0:T(8,128)(2,1)}, u32[]{:S(2)}, u32[]{:S(2)}) collective-permute-start(bf16[5200,128]{1,0:T(8,128)(2,1)} %get-tuple-element.47.lower_ref), channel_id=1, source_target_pairs={{1,0},{2,1},{3,2},{4,3},{5,4},{6,5},{7,6},{8,7},{9,8},{10,9},{11,1... | collective-permute-start | bytes 3993608 | tf_op jit(solution)/shard_map/ppermute | solution.py:995
  33.9 54.0 %collective-permute-start.3 = (bf16[5200,128]{1,0:T(8,128)(2,1)}, bf16[5200,128]{1,0:T(8,128)(2,1)S(1)}, u32[]{:S(2)}, u32[]{:S(2)}) collective-permute-start(bf16[5200,128]{1,0:T(8,128)(2,1)} %get-tuple-element.46.upper_ref), channel_id=1, source_target_pairs={{1,0},{2,1},{3,2},{4,3},{5,4},{6,5},{7,6},{8,7},{9,8},{10,9},{11,1... | collective-permute-start | bytes 3993608 | tf_op jit(solution)/shard_map/ppermute | solution.py:995
  35.8 52.1 %collective-permute-start.2 = (bf16[5200,128]{1,0:T(8,128)(2,1)}, bf16[5200,128]{1,0:T(8,128)(2,1)S(1)}, u32[]{:S(2)}, u32[]{:S(2)}) collective-permute-start(bf16[5200,128]{1,0:T(8,128)(2,1)} %get-tuple-element.47.lower_ref), channel_id=1, source_target_pairs={{0,1},{1,2},{2,3},{3,4},{4,5},{5,6},{6,7},{7,8},{8,9},{9,10},{10,1... | collective-permute-start | bytes 3993608 | tf_op jit(solution)/shard_map/ppermute | solution.py:995
  39.8 1.3 %copy-start.2 = (f32[2,40,32,128]{3,2,1,0:T(8,128)S(1)}, f32[2,40,32,128]{3,2,1,0:T(8,128)}, u32[]{:S(2)}) copy-start(f32[2,40,32,128]{3,2,1,0:T(8,128)} %vel_ref.3) | copy-start | bytes 3932164
  44.0 18.2 %copy-start.4 = (bf16[2,2,512]{2,1,0:T(2,128)(2,1)S(1)}, bf16[2,2,512]{2,1,0:T(2,128)(2,1)}, u32[]{:S(2)}) copy-start(bf16[2,2,512]{2,1,0:T(2,128)(2,1)} %param.14) | copy-start | bytes 12292
  99.2 20.4 %all-to-all-start.1 = ((f32[8,6,128]{2,1,0:T(8,128)}), f32[8,6,128]{2,1,0:T(8,128)S(1)}, u32[]{:S(2)}, u32[]{:S(2)}) async-start(f32[8,6,128]{2,1,0:T(8,128)} %get-tuple-element.61), calls=%async_computation.1 | async-start | bytes 65536 | tf_op jit(solution)/shard_map/all_to_all | solution.py:1030
